TPU v7x, 512 devices: a whole 4x8x8 slice. The times are simulated.
512 devices in a mesh: rep: 8 (over x, y_lo), fsdp: 64 (over z, y_hi, core).
Axes of the slice: x: 4, y: 8 (y_hi: 4, y_lo: 2; y = y_hi * 2 + y_lo), z: 8, core: 2. Of those that a mesh axis runs over, the one named last changes fastest.
Arguments:
- tokens_in: bfloat16 [8, 2048, 2048], P('rep', 'fsdp'), may hold values from -6 to 6
- out_grad: bfloat16 [8, 2048, 2048], P('rep', 'fsdp'), may hold values from -18 to 18
- gate_weight: bfloat16 [8, 4096, 2048], P('rep', 'fsdp'), may hold values from -6.1 to 6.1
- up_weight: bfloat16 [8, 4096, 2048], P('rep', 'fsdp'), may hold values from -6 to 6
- down_weight: bfloat16 [8, 4096, 2048], P('rep', 'fsdp'), may hold values from -20 to 20
- base_gate: bfloat16 [4096, 2048], P('fsdp'), may hold values from -6 to 6
- first_moment: float32 [8, 4096, 2048], P('rep', 'fsdp'), may hold values from -3 to 3
- second_moment: float32 [8, 4096, 2048], P('rep', 'fsdp'), may hold values from 0.05 to 1
- outer_momentum: float32 [4096, 2048], P('fsdp'), may hold values from -0.18 to 0.18
Outputs:
- new_base: float32 [4096, 2048], P('fsdp')
- new_momentum: float32 [4096, 2048], P('fsdp')
- first_out: float32 [8, 4096, 2048], P('rep', 'fsdp')
- second_out: float32 [8, 4096, 2048], P('rep', 'fsdp')
All inputs are finite; a program needn't handle non-finite values.
Results may differ from a plain program's by a relative error of at most 0.0033.
Values may be sent and summed in bfloat16 or wider, within the bound.
A program may use at most 64 MiB of HBM per device.

v0:
```python
import math

import jax
import jax.numpy as jnp
from jax import lax
from jax.sharding import PartitionSpec as P

inner_rate = 0.02
beta_first = 0.9
beta_second = 0.95
adam_floor = 1e-08
decay_rate = 0.1
bias_first = 1.0 - 0.9**20
bias_second = 1.0 - 0.95**20
nesterov_factor = 0.9
outer_rate = 0.7


def on_device(
    tokens_in,
    out_grad,
    gate_weight,
    up_weight,
    down_weight,
    base_gate,
    first_moment,
    second_moment,
    outer_momentum,
):
    rows = tokens_in[0]
    grads = out_grad[0]
    gate = gate_weight[0]
    down = down_weight[0]
    units = gate.shape[0]
    in_scale = 1.0 / math.sqrt(rows.shape[1])
    out_scale = 1.0 / math.sqrt(units * lax.axis_size("fsdp"))
    paired = jnp.concatenate([gate, up_weight[0]], axis=0)
    every_row = lax.all_gather(rows, "fsdp", axis=0, tiled=True)
    every_both = (
        jnp.einsum("td,fd->tf", every_row, paired, preferred_element_type=jnp.float32) * in_scale
    )
    pre = every_both[:, :units]
    lin = every_both[:, units:]
    back = (
        jnp.einsum(
            "td,fd->tf",
            lax.all_gather(grads, "fsdp", axis=0, tiled=True),
            down,
            preferred_element_type=jnp.float32,
        )
        * out_scale
    )
    sig = jax.nn.sigmoid(pre)
    dpre = (back * lin * sig * (1.0 + pre * (1.0 - sig))).astype(jnp.bfloat16)
    summed = jnp.einsum("tf,td->fd", dpre, every_row, preferred_element_type=jnp.float32)
    grad = summed * in_scale
    moment_new = beta_first * first_moment[0] + (1.0 - beta_first) * grad
    second_new = beta_second * second_moment[0] + (1.0 - beta_second) * grad * grad
    direction = moment_new / bias_first / (jnp.sqrt(second_new / bias_second) + adam_floor)
    inner = gate.astype(jnp.float32) * (1.0 - inner_rate * decay_rate) - inner_rate * direction
    base_value = base_gate.astype(jnp.float32)
    difference = base_value - inner
    groups = lax.axis_size("rep")
    total = lax.psum(difference, "rep")
    outer_grad = total / groups
    new_momentum = nesterov_factor * outer_momentum + outer_grad
    new_base = base_value - outer_rate * (outer_grad + nesterov_factor * new_momentum)
    return (new_base, new_momentum, moment_new[None], second_new[None])


def solution(mesh):
    in_specs = (
        P("rep", "fsdp", None),
        P("rep", "fsdp", None),
        P("rep", "fsdp", None),
        P("rep", "fsdp", None),
        P("rep", "fsdp", None),
        P("fsdp", None),
        P("rep", "fsdp", None),
        P("rep", "fsdp", None),
        P("fsdp", None),
    )
    out_specs = (P("fsdp", None), P("fsdp", None), P("rep", "fsdp", None), P("rep", "fsdp", None))
    return jax.shard_map(
        on_device, mesh=mesh, in_specs=in_specs, out_specs=out_specs, check_vma=False
    )
```

profile of v0, /device:TPU:16, one launch (start us, length us, event | category | flops | bytes accessed | tf_op | source)
XLA Modules:
  0.0 325.3 jit_solution(10408972838895187928)
XLA Ops:
  7.2 0.0 copy-start
  7.2 0.0 copy-start.2
  7.2 0.0 copy-start.3
  7.2 0.0 copy-start.4
  7.2 0.0 copy-start.5
  7.2 0.0 all-gather.7.cloned.1.call-start
  7.3 0.7 all-gather.7.cloned.1.call-update
  8.0 0.0 all-gather.5.cloned.1.call-start
  8.0 0.7 all-gather.5.cloned.1.call-update
  8.7 0.0 all-reduce.2.cloned.1.call-start
  8.8 109.4 %all-gather.7.cloned.1.call-done = bf16[1,2048,2048]{2,1,0:T(8,128)(2,1)} async-done(((bf16[1,32,2048]{2,1,0:T(8,128)(2,1)}), bf16[1,2048,2048]{2,1,0:T(8,128)(2,1)}) %all-gather.7.cloned.1.call-update) | async-done | bytes 8388624 | tf_op jit(solution)/shard_map/all_gather | solution.py:38
  118.2 6.5 %fusion.9 = f32[2048,128]{0,1:T(8,128)S(1)} fusion(bf16[1,2048,2048]{2,1,0:T(8,128)(2,1)} %all-gather.7.cloned.1.call-done, bf16[64,2048]{1,0:T(8,128)(2,1)} %bitcast.55, bf16[64,2048]{1,0:T(8,128)(2,1)} %bitcast.56), kind=kOutput, calls=%fused_computation.7 | convolution fusion | flops 1075052544 | bytes 9961472 | tf_op jit(solution)/shard_map/td,fd->tf/dot_general | solution.py:40
  124.6 0.0 copy-start.1
  124.7 96.8 %all-gather.5.cloned.1.call-done = bf16[1,2048,2048]{2,1,0:T(8,128)(2,1)} async-done(((bf16[1,32,2048]{2,1,0:T(8,128)(2,1)}), bf16[1,2048,2048]{2,1,0:T(8,128)(2,1)}) %all-gather.5.cloned.1.call-update) | async-done | bytes 8388624 | tf_op jit(solution)/shard_map/all_gather | solution.py:47
  221.5 0.0 copy-done
  221.5 0.0 copy-done.2
  221.5 0.0 copy-done.3
  221.5 0.0 copy-done.4
  221.5 0.0 copy-done.5
  221.5 11.5 %fusion.46 = (f32[1,64,2048]{2,1,0:T(8,128)}, f32[64,2048]{1,0:T(8,128)}, f32[1,64,2048]{2,1,0:T(8,128)}) fusion(f32[1,64,2048]{2,1,0:T(8,128)S(1)} %copy-done.4, f32[1,64,2048]{2,1,0:T(8,128)S(1)} %copy-done.5, bf16[1,64,2048]{2,1,0:T(8,128)(2,1)S(1)} %copy-done.2, bf16[64,2048]{1,0:T(8,128)(2,1)S(1)} %copy-done.3, ...), kind=kOutput, calls=%fused_computation.34 | convolution fusion | flops 1077542912 | bytes 21233664 | tf_op jit(solution)/shard_map/tf,td->fd/dot_general | solution.py:55
  233.0 0.0 all-reduce.2.cloned.1.call-update
  233.0 83.6 %all-reduce.2.cloned.1.call-done = f32[64,2048]{1,0:T(8,128)} async-done(((f32[64,2048]{1,0:T(8,128)}), f32[64,2048]{1,0:T(8,128)}) %all-reduce.2.cloned.1.call-update) | async-done | bytes 524304 | tf_op jit(solution)/shard_map/psum | solution.py:64
  316.6 0.0 copy-done.1
  316.6 2.1 convert_subtract_fusion
Async XLA Ops:
  7.2 214.3 %copy-start = (bf16[1,64,2048]{2,1,0:T(8,128)(2,1)S(1)}, bf16[1,64,2048]{2,1,0:T(8,128)(2,1)}, u32[]{:S(2)}) copy-start(bf16[1,64,2048]{2,1,0:T(8,128)(2,1)} %param.13) | copy-start | bytes 786436
  7.2 214.3 %copy-start.2 = (bf16[1,64,2048]{2,1,0:T(8,128)(2,1)S(1)}, bf16[1,64,2048]{2,1,0:T(8,128)(2,1)}, u32[]{:S(2)}) copy-start(bf16[1,64,2048]{2,1,0:T(8,128)(2,1)} %param.11) | copy-start | bytes 786436
  7.2 214.3 %copy-start.3 = (bf16[64,2048]{1,0:T(8,128)(2,1)S(1)}, bf16[64,2048]{1,0:T(8,128)(2,1)}, u32[]{:S(2)}) copy-start(bf16[64,2048]{1,0:T(8,128)(2,1)} %param.14) | copy-start | bytes 786436
  7.2 214.3 %copy-start.4 = (f32[1,64,2048]{2,1,0:T(8,128)S(1)}, f32[1,64,2048]{2,1,0:T(8,128)}, u32[]{:S(2)}) copy-start(f32[1,64,2048]{2,1,0:T(8,128)} %param.16) | copy-start | bytes 1572868
  7.2 214.3 %copy-start.5 = (f32[1,64,2048]{2,1,0:T(8,128)S(1)}, f32[1,64,2048]{2,1,0:T(8,128)}, u32[]{:S(2)}) copy-start(f32[1,64,2048]{2,1,0:T(8,128)} %param.15) | copy-start | bytes 1572868
  7.2 111.0 %all-gather.7.cloned.1.call-start = ((), (), s32[]{:S(2)}) async-start(), calls=%async_computation.2 | async-start | bytes 8519680 | tf_op jit(solution)/shard_map/all_gather | solution.py:38
  8.0 213.5 %all-gather.5.cloned.1.call-start = ((), (), s32[]{:S(2)}) async-start(), calls=%async_computation.1 | async-start | bytes 8519680 | tf_op jit(solution)/shard_map/all_gather | solution.py:47
  8.7 307.9 %all-reduce.2.cloned.1.call-start = ((), (), s32[]{:S(2)}) async-start(), calls=%async_computation | async-start | bytes 1048576 | tf_op jit(solution)/shard_map/psum | solution.py:64
  124.6 191.9 %copy-start.1 = (f32[64,2048]{1,0:T(8,128)S(1)}, f32[64,2048]{1,0:T(8,128)}, u32[]{:S(2)}) copy-start(f32[64,2048]{1,0:T(8,128)} %param.17) | copy-start | bytes 1572868
Sparse Core Ops, SparseCore 0:
  11.4 106.7 all-gather.6
  121.5 99.9 all-gather.4
  233.1 83.4 all-reduce.1
where the time goes:
time: 325 us
  waiting for transfers between devices  291 us (90%)
  matrix products  17.9 us (6%)
  between operations  13.8 us (4%)
    all_gather x1, waiting for transfers between devices, on_device(): every_row = lax.all_gather(rows, 'fsdp', axis=0, tiled=True)  109 us
    all_gather x1, waiting for transfers between devices, on_device(): lax.all_gather(grads, 'fsdp', axis=0, tiled=True)  96.8 us
    psum x1, waiting for transfers between devices, on_device(): total = lax.psum(difference, 'rep')  83.6 us
    dot_general x1, matrix products, on_device(): jnp.einsum('tf,td->fd', dpre, every_row, preferred_element_type=jnp.float32)  11.5 us
  transfers between devices with their start and end apart: 3, of which 3 were waited for; matrix products, arithmetic and copies ran while one was open for 2% of the time, Pallas kernels for 0%

commit v1 on v0

v1 whole, which is shorter than its diff:
```python
import math

import jax
import jax.numpy as jnp
from jax import lax
from jax.experimental import pallas as pl
from jax.experimental.pallas import tpu as pltpu
from jax.sharding import PartitionSpec as P

inner_rate = 0.02
beta_first = 0.9
beta_second = 0.95
adam_floor = 1e-08
decay_rate = 0.1
bias_first = 1.0 - 0.9**20
bias_second = 1.0 - 0.95**20
nesterov_factor = 0.9
outer_rate = 0.7

MESH = pl.DeviceIdType.MESH
NZ, NY, REP = 8, 4, 8
ROWS, UNITS, D = 32, 64, 2048
SLOT = 4 * ROWS
CHUNK = 16
N_CHUNK = UNITS // CHUNK
COLS = D // REP

in_scale = 1.0 / math.sqrt(D)
out_scale = 1.0 / math.sqrt(UNITS * NZ * NY * 2)


def place(way, hops):
    if hops == 0:
        return 0
    if hops == NZ // 2:
        return 1
    return 2 * hops + way


def kernel(
    tokens, grads, gate, up, down, base, first, second,
    grad_out, total_out,
    xg, wp, wd, acc, base_v, first_v, second_v, gsend, grecv, grad_v, diff, rs, ag,
    load_sem, zs, zr, cs, cr, ys, yr, ws, wr, gs, gr, ss, sr, as_, ar, out_sem,
):
    rep = lax.axis_index("rep")
    me = lax.axis_index("fsdp")
    z = me // (2 * NY)
    y = (me // 2) % NY
    core = me % 2

    def at(z_, y_, core_):
        return (rep, (z_ * NY + y_) * 2 + core_)

    z_next = (at((z + 1) % NZ, y, core), at((z + NZ - 1) % NZ, y, core))
    sibling = at(z, y, 1 - core)
    token_pair = at(z, y + 1 - 2 * (y % 2), core)
    weight_pair = at(z, (y + 3 + 2 * (y % 2)) % NY, core)
    peers = [((rep + k) % REP, me) for k in range(1, REP)]

    loads = [
        pltpu.make_async_copy(src, dst, load_sem.at[i])
        for i, (src, dst) in enumerate(
            [
                (tokens.at[0], xg.at[0, pl.ds(0, ROWS)]),
                (grads.at[0], xg.at[1, pl.ds(0, ROWS)]),
                (gate.at[0], wp.at[pl.ds(0, UNITS)]),
                (up.at[0], wp.at[pl.ds(2 * UNITS, UNITS)]),
                (down.at[0], wd.at[pl.ds(0, UNITS)]),
                (base, base_v),
                (first.at[0], first_v),
                (second.at[0], second_v),
            ]
        )
    ]
    for load in loads:
        load.start()

    barrier = pltpu.get_barrier_semaphore()
    others = [*z_next, sibling, token_pair, weight_pair, *peers]
    for other in others:
        pl.semaphore_signal(barrier, inc=1, device_id=other, device_id_type=MESH)
    for load in loads[:5]:
        load.wait()
    pl.semaphore_wait(barrier, len(others))

    def remote(src, dst, send, recv, device):
        return pltpu.make_async_remote_copy(
            src_ref=src, dst_ref=dst, send_sem=send, recv_sem=recv, device_id=device, device_id_type=MESH
        )

    def shard(kind, slot, yy, cc):
        return xg.at[kind, pl.ds(slot * SLOT + yy * 2 * ROWS + cc * ROWS, ROWS)]

    def z_copy(way, yy, hops, kind):
        return remote(
            shard(kind, place(way, hops - 1), yy, 0),
            shard(kind, place(way, hops), yy, 0),
            zs.at[way, yy, hops - 1, kind],
            zr.at[way, yy, hops - 1, kind],
            z_next[way],
        )

    def core_copy(slot, yy, kind):
        return remote(
            shard(kind, slot, yy, 0), shard(kind, slot, yy, 1), cs.at[slot, yy, kind], cr.at[slot, yy, kind], sibling
        )

    def y_copy(kind):
        return remote(shard(kind, 0, 0, 0), shard(kind, 0, 1, 0), ys.at[kind], yr.at[kind], token_pair)

    def w_copy(i):
        ref, row = ((wp, 0), (wp, 2 * UNITS), (wd, 0))[i]
        return remote(
            ref.at[pl.ds(row, UNITS)], ref.at[pl.ds(row + UNITS, UNITS)], ws.at[i], wr.at[i], weight_pair
        )

    sent = []

    def start(copy):
        copy.start()
        sent.append(copy)

    for kind in range(2):
        start(y_copy(kind))
        for way in range(2):
            start(z_copy(way, 0, 1, kind))
    for i in range(3):
        start(w_copy(i))
    for kind in range(2):
        start(core_copy(0, 0, kind))

    def arrive(yy, hops):
        for kind in range(2):
            for way in range(2):
                if hops == NZ // 2 and kind != way:
                    continue
                z_copy(way, yy, hops, kind).wait_recv()
                if hops + 1 < NZ // 2 or (hops + 1 == NZ // 2 and kind == way):
                    start(z_copy(way, yy, hops + 1, kind))
                start(core_copy(place(way, hops), yy, kind))

    arrive(0, 1)
    arrive(0, 2)
    for kind in range(2):
        y_copy(kind).wait_recv()
        for way in range(2):
            start(z_copy(way, 1, 1, kind))
        start(core_copy(0, 1, kind))
    arrive(1, 1)
    arrive(0, 3)
    arrive(1, 2)
    arrive(0, 4)
    arrive(1, 3)

    nt = (((1,), (1,)), ((), ()))

    def block(slot, slots, begin):
        for s in range(slot, slot + slots):
            for yy in range(2):
                for kind in range(2):
                    core_copy(s, yy, kind).wait_recv()
        rows = pl.ds(slot * SLOT, slots * SLOT)
        x = xg[0, rows]
        both = lax.dot_general(wp[...], x, nt, preferred_element_type=jnp.float32) * in_scale
        pre, lin = both[: 2 * UNITS], both[2 * UNITS :]
        back = lax.dot_general(wd[...], xg[1, rows], nt, preferred_element_type=jnp.float32) * out_scale
        sig = jax.nn.sigmoid(pre)
        dpre = (back * lin * sig * (1.0 + pre * (1.0 - sig))).astype(jnp.bfloat16)
        part = jnp.dot(dpre, x, preferred_element_type=jnp.float32)
        if begin:
            acc[...] = part
        else:
            acc[...] += part

    for i in range(3):
        w_copy(i).wait_recv()
    block(0, 1, True)
    block(2, 2, False)
    block(4, 2, False)
    block(6, 2, False)
    arrive(1, 4)
    block(1, 1, False)

    def g_copy(c):
        rows = pl.ds(c * CHUNK, CHUNK)
        return remote(gsend.at[rows], grecv.at[rows], gs.at[c], gr.at[c], weight_pair)

    for c in range(N_CHUNK):
        gsend[pl.ds(c * CHUNK, CHUNK)] = acc[pl.ds(UNITS + c * CHUNK, CHUNK)].astype(jnp.bfloat16)
        start(g_copy(c))
    for load in loads[5:]:
        load.wait()

    mine = pl.ds(pl.multiple_of(rep * COLS, COLS), COLS)

    def rs_copy(c, k):
        rows = pl.ds(c * CHUNK, CHUNK)
        cols = pl.ds(pl.multiple_of(((rep + k) % REP) * COLS, COLS), COLS)
        return remote(diff.at[rows, cols], rs.at[k - 1, rows], ss.at[c, k - 1], sr.at[c, k - 1], peers[k - 1])

    def ag_copy(c, k):
        rows = pl.ds(c * CHUNK, CHUNK)
        return remote(ag.at[rows, mine], ag.at[rows, mine], as_.at[c, k - 1], ar.at[c, k - 1], peers[k - 1])

    outs = []

    def sum_chunk(c):
        rows = pl.ds(c * CHUNK, CHUNK)
        total = diff[rows, mine]
        for k in range(1, REP):
            rs_copy(c, k).wait_recv()
            total += rs[k - 1, rows]
        ag[rows, mine] = total / REP
        for k in range(1, REP):
            start(ag_copy(c, k))

    for c in range(N_CHUNK):
        rows = pl.ds(c * CHUNK, CHUNK)
        g_copy(c).wait_recv()
        grad = (acc[rows] + grecv[rows].astype(jnp.float32)) * in_scale
        grad_v[rows] = grad
        moment_new = beta_first * first_v[rows] + (1.0 - beta_first) * grad
        second_new = beta_second * second_v[rows] + (1.0 - beta_second) * grad * grad
        direction = moment_new / bias_first / (jnp.sqrt(second_new / bias_second) + adam_floor)
        gate_value = wp[rows].astype(jnp.float32)
        inner = gate_value * (1.0 - inner_rate * decay_rate) - inner_rate * direction
        diff[rows] = base_v[rows].astype(jnp.float32) - inner
        for k in range(1, REP):
            start(rs_copy(c, k))
        out = pltpu.make_async_copy(grad_v.at[rows], grad_out.at[rows], out_sem.at[0, c])
        out.start()
        outs.append(out)
        if c > 0:
            sum_chunk(c - 1)
    sum_chunk(N_CHUNK - 1)

    for c in range(N_CHUNK):
        rows = pl.ds(c * CHUNK, CHUNK)
        for k in range(1, REP):
            ag_copy(c, k).wait_recv()
        out = pltpu.make_async_copy(ag.at[rows], total_out.at[rows], out_sem.at[1, c])
        out.start()
        outs.append(out)
    for copy in sent:
        copy.wait_send()
    for out in outs:
        out.wait()


def on_device(
    tokens_in,
    out_grad,
    gate_weight,
    up_weight,
    down_weight,
    base_gate,
    first_moment,
    second_moment,
    outer_momentum,
):
    dma = pltpu.SemaphoreType.DMA
    f32, bf16 = jnp.float32, jnp.bfloat16
    grad, outer_grad = pl.pallas_call(
        kernel,
        out_shape=[jax.ShapeDtypeStruct((UNITS, D), f32)] * 2,
        in_specs=[pl.BlockSpec(memory_space=pl.ANY)] * 8,
        out_specs=[pl.BlockSpec(memory_space=pl.ANY)] * 2,
        scratch_shapes=[
            pltpu.VMEM((2, NZ * SLOT, D), bf16),
            pltpu.VMEM((4 * UNITS, D), bf16),
            pltpu.VMEM((2 * UNITS, D), bf16),
            pltpu.VMEM((2 * UNITS, D), f32),
            pltpu.VMEM((UNITS, D), bf16),
            pltpu.VMEM((UNITS, D), f32),
            pltpu.VMEM((UNITS, D), f32),
            pltpu.VMEM((UNITS, D), bf16),
            pltpu.VMEM((UNITS, D), bf16),
            pltpu.VMEM((UNITS, D), f32),
            pltpu.VMEM((UNITS, D), f32),
            pltpu.VMEM((REP - 1, UNITS, COLS), f32),
            pltpu.VMEM((UNITS, D), f32),
            dma((8,)),
            dma((2, 2, NZ // 2, 2)),
            dma((2, 2, NZ // 2, 2)),
            dma((NZ, 2, 2)),
            dma((NZ, 2, 2)),
            dma((2,)),
            dma((2,)),
            dma((3,)),
            dma((3,)),
            dma((N_CHUNK,)),
            dma((N_CHUNK,)),
            dma((N_CHUNK, REP - 1)),
            dma((N_CHUNK, REP - 1)),
            dma((N_CHUNK, REP - 1)),
            dma((N_CHUNK, REP - 1)),
            dma((2, N_CHUNK)),
        ],
        compiler_params=pltpu.CompilerParams(
            collective_id=0, has_side_effects=True, vmem_limit_bytes=48 * 2**20
        ),
        name="window",
    )(
        tokens_in,
        out_grad,
        gate_weight,
        up_weight,
        down_weight,
        base_gate,
        first_moment,
        second_moment,
    )
    moment_new = beta_first * first_moment[0] + (1.0 - beta_first) * grad
    second_new = beta_second * second_moment[0] + (1.0 - beta_second) * grad * grad
    new_momentum = nesterov_factor * outer_momentum + outer_grad
    base_value = base_gate.astype(jnp.float32)
    new_base = base_value - outer_rate * (outer_grad + nesterov_factor * new_momentum)
    return (new_base, new_momentum, moment_new[None], second_new[None])


def solution(mesh):
    in_specs = (
        P("rep", "fsdp", None),
        P("rep", "fsdp", None),
        P("rep", "fsdp", None),
        P("rep", "fsdp", None),
        P("rep", "fsdp", None),
        P("fsdp", None),
        P("rep", "fsdp", None),
        P("rep", "fsdp", None),
        P("fsdp", None),
    )
    out_specs = (P("fsdp", None), P("fsdp", None), P("rep", "fsdp", None), P("rep", "fsdp", None))
    return jax.shard_map(
        on_device, mesh=mesh, in_specs=in_specs, out_specs=out_specs, check_vma=False
    )
```

time: 325 us -> 101 us (0.31)
  the two profiles are of different devices: /device:TPU:16 before, /device:TPU:8 now
where the time goes in v1:
time: 101 us
  Pallas kernels  90 us (89%)
  local copies, waits for them, and re-layouts  7.68 us (8%)
  other arithmetic  2.22 us (2%)
    pallas_call x1, Pallas kernels, on_device(): pl.pallas_call(kernel, out_shape=[jax.ShapeDtypeStruct((UNITS, D), f32)]...  90 us
    unnamed x18, local copies, waits for them, and re-layouts  7.68 us

profile of v1, /device:TPU:8, one launch (start us, length us, event | category | flops | bytes accessed | tf_op | source)
XLA Modules:
  0.0 100.6 jit_solution(1703734382517173453)
XLA Ops:
  0.6 0.0 copy-start
  0.6 1.0 %copy-done = f32[1,64,2048]{2,1,0:T(8,128)S(1)} copy-done((f32[1,64,2048]{2,1,0:T(8,128)S(1)}, f32[1,64,2048]{2,1,0:T(8,128)}, u32[]{:S(2)}) %copy-start) | copy-done | bytes 524312
  1.7 0.0 copy-start.1
  1.7 1.0 %copy-done.1 = f32[1,64,2048]{2,1,0:T(8,128)S(1)} copy-done((f32[1,64,2048]{2,1,0:T(8,128)S(1)}, f32[1,64,2048]{2,1,0:T(8,128)}, u32[]{:S(2)}) %copy-start.1) | copy-done | bytes 524312
  2.7 0.0 copy-start.2
  2.7 0.9 copy-done.2
  3.7 0.0 copy-start.3
  3.7 0.9 copy-done.3
  4.6 0.0 copy-start.4
  4.6 0.9 copy-done.4
  5.6 0.0 copy-start.5
  5.6 0.9 copy-done.5
  6.5 0.0 copy-start.6
  6.5 0.9 copy-done.6
  7.4 0.0 copy-start.7
  7.4 0.9 copy-done.7
  8.3 0.0 copy-start.8
  8.3 90.0 %window.1 = (f32[64,2048]{1,0:T(8,128)S(1)}, f32[64,2048]{1,0:T(8,128)S(1)}) custom-call(bf16[1,32,2048]{2,1,0:T(8,128)(2,1)S(1)} %copy-done.6, bf16[1,32,2048]{2,1,0:T(8,128)(2,1)S(1)} %copy-done.7, bf16[1,64,2048]{2,1,0:T(8,128)(2,1)S(1)} %copy-done.3, bf16[1,64,2048]{2,1,0:T(8,128)(2,1)S(1)} %copy-done.4, bf16[1,64,2048]{2,1,0:T(8,128)(2,1)S(1)} %copy-done.5, ...), custom_call_target="tpu_custom_call" | custom-call | tf_op jit(solution)/shard_map/window/pallas_call | solution.py:264
  98.4 0.0 copy-done.8
  98.4 1.1 %multiply_subtract_fusion = (f32[64,2048]{1,0:T(8,128)}, f32[64,2048]{1,0:T(8,128)}) fusion(f32[64,2048]{1,0:T(8,128)S(1)} %get-tuple-element.6, bf16[64,2048]{1,0:T(8,128)(2,1)S(1)} %copy-done.2, f32[64,2048]{1,0:T(8,128)S(1)} %copy-done.8), kind=kLoop, calls=%fused_computation.5 | loop fusion | flops 917504 | bytes 2359296 | tf_op jit(solution)/shard_map/sub | solution.py:318
  99.5 1.1 %fusion.1 = (f32[1,64,2048]{2,1,0:T(8,128)}, f32[1,64,2048]{2,1,0:T(8,128)}) fusion(f32[64,2048]{1,0:T(8,128)S(1)} %get-tuple-element.7, f32[1,64,2048]{2,1,0:T(8,128)S(1)} %copy-done.1, f32[1,64,2048]{2,1,0:T(8,128)S(1)} %copy-done), kind=kLoop, calls=%fused_computation.2 | loop fusion | flops 917504 | bytes 2621440 | tf_op jit(solution)/shard_map/broadcast_in_dim | solution.py:319
Async XLA Ops:
  0.6 1.0 %copy-start = (f32[1,64,2048]{2,1,0:T(8,128)S(1)}, f32[1,64,2048]{2,1,0:T(8,128)}, u32[]{:S(2)}) copy-start(f32[1,64,2048]{2,1,0:T(8,128)} %first.1) | copy-start | bytes 1572868
  1.7 1.0 %copy-start.1 = (f32[1,64,2048]{2,1,0:T(8,128)S(1)}, f32[1,64,2048]{2,1,0:T(8,128)}, u32[]{:S(2)}) copy-start(f32[1,64,2048]{2,1,0:T(8,128)} %second.1) | copy-start | bytes 1572868
  2.7 0.9 copy-start.2
  3.7 0.9 copy-start.3
  4.6 0.9 copy-start.4
  5.6 0.9 copy-start.5
  6.5 0.9 copy-start.6
  7.4 0.9 copy-start.7
  8.3 90.0 %copy-start.8 = (f32[64,2048]{1,0:T(8,128)S(1)}, f32[64,2048]{1,0:T(8,128)}, u32[]{:S(2)}) copy-start(f32[64,2048]{1,0:T(8,128)} %param.17) | copy-start | bytes 1572868

commit v2 on v1

v2 whole, which is shorter than its diff:
```python
import math

import jax
import jax.numpy as jnp
from jax import lax
from jax.experimental import pallas as pl
from jax.experimental.pallas import tpu as pltpu
from jax.sharding import PartitionSpec as P

inner_rate = 0.02
beta_first = 0.9
beta_second = 0.95
adam_floor = 1e-08
decay_rate = 0.1
bias_first = 1.0 - 0.9**20
bias_second = 1.0 - 0.95**20
nesterov_factor = 0.9
outer_rate = 0.7

MESH = pl.DeviceIdType.MESH
NZ, NY, REP = 8, 4, 8
ROWS, UNITS, D = 32, 64, 2048
SLOT = 4 * ROWS
CHUNK = 16
N_CHUNK = UNITS // CHUNK
COLS = D // REP

in_scale = 1.0 / math.sqrt(D)
out_scale = 1.0 / math.sqrt(UNITS * NZ * NY * 2)


def place(way, hops):
    if hops == 0:
        return 0
    if hops == NZ // 2:
        return 1
    return 2 * hops + way


def kernel(
    tokens, grads, gate, up, down, base, first, second,
    grad_out, total_out,
    xg, wp, wd, acc, base_v, first_v, second_v, gsend, grecv, grad_v, diff, diff_b, rs, ag,
    load_sem, zs, zr, cs, cr, ys, yr, ws, wr, gs, gr, ss, sr, as_, ar, out_sem,
):
    rep = lax.axis_index("rep")
    me = lax.axis_index("fsdp")
    z = me // (2 * NY)
    y = (me // 2) % NY
    core = me % 2

    def at(z_, y_, core_):
        return (rep, (z_ * NY + y_) * 2 + core_)

    z_next = (at((z + 1) % NZ, y, core), at((z + NZ - 1) % NZ, y, core))
    sibling = at(z, y, 1 - core)
    token_pair = at(z, y + 1 - 2 * (y % 2), core)
    weight_pair = at(z, (y + 3 + 2 * (y % 2)) % NY, core)
    peers = [((rep + k) % REP, me) for k in range(1, REP)]

    loads = [
        pltpu.make_async_copy(src, dst, load_sem.at[i])
        for src, dst, i in [
            (tokens.at[0], xg.at[0, pl.ds(0, ROWS)], 0),
            (grads.at[0], xg.at[1, pl.ds(0, ROWS)], 0),
            (gate.at[0], wp.at[pl.ds(0, UNITS)], 0),
            (up.at[0], wp.at[pl.ds(2 * UNITS, UNITS)], 0),
            (down.at[0], wd.at[pl.ds(0, UNITS)], 0),
            (base, base_v, 1),
            (first.at[0], first_v, 2),
            (second.at[0], second_v, 3),
        ]
    ]
    for load in loads:
        load.start()

    barrier = pltpu.get_barrier_semaphore()
    others = [*z_next, sibling, token_pair, weight_pair, *peers]
    for other in others:
        pl.semaphore_signal(barrier, inc=1, device_id=other, device_id_type=MESH)
    pltpu.make_async_copy(wp, wp, load_sem.at[0]).wait()
    pl.semaphore_wait(barrier, len(others))

    def remote(src, dst, send, recv, device):
        return pltpu.make_async_remote_copy(
            src_ref=src, dst_ref=dst, send_sem=send, recv_sem=recv, device_id=device, device_id_type=MESH
        )

    def wait_bytes(ref, sem):
        pltpu.make_async_copy(ref, ref, sem).wait()

    def shard(kind, slot, yy, cc):
        return xg.at[kind, pl.ds(slot * SLOT + yy * 2 * ROWS + cc * ROWS, ROWS)]

    def z_copy(way, yy, hops, kind):
        return remote(
            shard(kind, place(way, hops - 1), yy, 0),
            shard(kind, place(way, hops), yy, 0),
            zs,
            zr.at[way, yy, hops - 1, kind],
            z_next[way],
        )

    def core_copy(slot, yy, kind):
        return remote(shard(kind, slot, yy, 0), shard(kind, slot, yy, 1), cs, cr.at[slot], sibling)

    def y_copy(kind):
        return remote(shard(kind, 0, 0, 0), shard(kind, 0, 1, 0), ys, yr.at[kind], token_pair)

    def w_copy(i):
        ref, row = ((wp, 0), (wp, 2 * UNITS), (wd, 0))[i]
        return remote(ref.at[pl.ds(row, UNITS)], ref.at[pl.ds(row + UNITS, UNITS)], ws, wr, weight_pair)

    for kind in range(2):
        y_copy(kind).start()
        for way in range(2):
            z_copy(way, 0, 1, kind).start()
    for i in range(3):
        w_copy(i).start()
    for kind in range(2):
        core_copy(0, 0, kind).start()

    def arrive(yy, hops):
        for kind in range(2):
            for way in range(2):
                if hops == NZ // 2 and kind != way:
                    continue
                z_copy(way, yy, hops, kind).wait_recv()
                if hops + 1 < NZ // 2 or (hops + 1 == NZ // 2 and kind == way):
                    z_copy(way, yy, hops + 1, kind).start()
                core_copy(place(way, hops), yy, kind).start()

    nt = (((1,), (1,)), ((), ()))

    def slopes(slot, slots):
        for s in range(slot, slot + slots):
            wait_bytes(xg.at[0, pl.ds(0, SLOT)], cr.at[s])
        rows = pl.ds(slot * SLOT, slots * SLOT)
        x = xg[0, rows]
        both = lax.dot_general(wp[...], x, nt, preferred_element_type=jnp.float32) * in_scale
        pre, lin = both[: 2 * UNITS], both[2 * UNITS :]
        back = lax.dot_general(wd[...], xg[1, rows], nt, preferred_element_type=jnp.float32) * out_scale
        sig = jax.nn.sigmoid(pre)
        return (back * lin * sig * (1.0 + pre * (1.0 - sig))).astype(jnp.bfloat16), x

    def block(slot, slots, begin=False):
        dpre, x = slopes(slot, slots)
        part = jnp.dot(dpre, x, preferred_element_type=jnp.float32)
        if begin:
            acc[...] = part
        else:
            acc[...] += part

    arrive(0, 1)
    arrive(0, 2)
    for kind in range(2):
        y_copy(kind).wait_recv()
        for way in range(2):
            z_copy(way, 1, 1, kind).start()
        core_copy(0, 1, kind).start()
    arrive(1, 1)
    arrive(0, 3)
    arrive(1, 2)
    arrive(0, 4)
    wait_bytes(wp.at[pl.ds(0, 3 * UNITS)], wr)
    block(0, 1, True)
    block(2, 2)
    block(4, 2)
    arrive(1, 3)
    block(6, 2)
    arrive(1, 4)

    def g_copy(c):
        rows = pl.ds(c * CHUNK, CHUNK)
        return remote(gsend.at[rows], grecv.at[rows], gs, gr.at[c], weight_pair)

    dpre, x = slopes(1, 1)
    part = jnp.dot(dpre[UNITS:], x, preferred_element_type=jnp.float32)
    gsend[...] = (acc[pl.ds(UNITS, UNITS)] + part).astype(jnp.bfloat16)
    for c in range(N_CHUNK):
        g_copy(c).start()
    acc[pl.ds(0, UNITS)] += jnp.dot(dpre[:UNITS], x, preferred_element_type=jnp.float32)
    for load in loads[5:]:
        load.wait()

    mine = pl.ds(pl.multiple_of(rep * COLS, COLS), COLS)

    def rs_copy(c, k):
        rows = pl.ds(c * CHUNK, CHUNK)
        cols = pl.ds(pl.multiple_of(((rep + k) % REP) * COLS, COLS), COLS)
        return remote(diff_b.at[rows, cols], rs.at[k - 1, rows], ss, sr.at[c], peers[k - 1])

    def ag_copy(c, k):
        rows = pl.ds(c * CHUNK, CHUNK)
        return remote(ag.at[rows, mine], ag.at[rows, mine], as_, ar.at[c], peers[k - 1])

    def sum_chunk(c):
        rows = pl.ds(c * CHUNK, CHUNK)
        wait_bytes(rs.at[:, rows], sr.at[c])
        total = diff[rows, mine]
        for k in range(1, REP):
            total += rs[k - 1, rows].astype(jnp.float32)
        ag[rows, mine] = (total / REP).astype(jnp.bfloat16)
        for k in range(1, REP):
            ag_copy(c, k).start()

    for c in range(N_CHUNK):
        rows = pl.ds(c * CHUNK, CHUNK)
        g_copy(c).wait_recv()
        grad = (acc[rows] + grecv[rows].astype(jnp.float32)) * in_scale
        grad_v[rows] = grad
        moment_new = beta_first * first_v[rows] + (1.0 - beta_first) * grad
        second_new = beta_second * second_v[rows] + (1.0 - beta_second) * grad * grad
        direction = moment_new / bias_first / (jnp.sqrt(second_new / bias_second) + adam_floor)
        gate_value = wp[rows].astype(jnp.float32)
        inner = gate_value * (1.0 - inner_rate * decay_rate) - inner_rate * direction
        difference = base_v[rows].astype(jnp.float32) - inner
        diff[rows] = difference
        diff_b[rows] = difference.astype(jnp.bfloat16)
        for k in range(1, REP):
            rs_copy(c, k).start()
        pltpu.make_async_copy(grad_v.at[rows], grad_out.at[rows], out_sem.at[0]).start()
        if c > 0:
            sum_chunk(c - 1)
    sum_chunk(N_CHUNK - 1)

    for c in range(N_CHUNK):
        rows = pl.ds(c * CHUNK, CHUNK)
        wait_bytes(ag.at[rows, pl.ds(0, D - COLS)], ar.at[c])
        pltpu.make_async_copy(ag.at[rows], total_out.at[rows], out_sem.at[1]).start()

    wait_bytes(xg.at[0, pl.ds(0, 28 * ROWS)], zs)
    wait_bytes(xg.at[0], cs)
    wait_bytes(xg.at[0, pl.ds(0, 2 * ROWS)], ys)
    wait_bytes(wp.at[pl.ds(0, 3 * UNITS)], ws)
    wait_bytes(gsend, gs)
    wait_bytes(diff_b.at[:, pl.ds(0, D - COLS)], ss)
    wait_bytes(diff_b.at[:, pl.ds(0, D - COLS)], as_)
    wait_bytes(grad_v, out_sem.at[0])
    wait_bytes(ag, out_sem.at[1])


def on_device(
    tokens_in,
    out_grad,
    gate_weight,
    up_weight,
    down_weight,
    base_gate,
    first_moment,
    second_moment,
    outer_momentum,
):
    dma = pltpu.SemaphoreType.DMA
    f32, bf16 = jnp.float32, jnp.bfloat16
    grad, total = pl.pallas_call(
        kernel,
        out_shape=[jax.ShapeDtypeStruct((UNITS, D), f32), jax.ShapeDtypeStruct((UNITS, D), bf16)],
        in_specs=[pl.BlockSpec(memory_space=pl.ANY)] * 8,
        out_specs=[pl.BlockSpec(memory_space=pl.ANY)] * 2,
        scratch_shapes=[
            pltpu.VMEM((2, NZ * SLOT, D), bf16),
            pltpu.VMEM((4 * UNITS, D), bf16),
            pltpu.VMEM((2 * UNITS, D), bf16),
            pltpu.VMEM((2 * UNITS, D), f32),
            pltpu.VMEM((UNITS, D), bf16),
            pltpu.VMEM((UNITS, D), f32),
            pltpu.VMEM((UNITS, D), f32),
            pltpu.VMEM((UNITS, D), bf16),
            pltpu.VMEM((UNITS, D), bf16),
            pltpu.VMEM((UNITS, D), f32),
            pltpu.VMEM((UNITS, D), f32),
            pltpu.VMEM((UNITS, D), bf16),
            pltpu.VMEM((REP - 1, UNITS, COLS), bf16),
            pltpu.VMEM((UNITS, D), bf16),
            dma((4,)),
            dma,
            dma((2, 2, NZ // 2, 2)),
            dma,
            dma((NZ,)),
            dma,
            dma((2,)),
            dma,
            dma,
            dma,
            dma((N_CHUNK,)),
            dma,
            dma((N_CHUNK,)),
            dma,
            dma((N_CHUNK,)),
            dma((2,)),
        ],
        compiler_params=pltpu.CompilerParams(
            collective_id=0, has_side_effects=True, vmem_limit_bytes=60 * 2**20
        ),
        name="window",
    )(
        tokens_in,
        out_grad,
        gate_weight,
        up_weight,
        down_weight,
        base_gate,
        first_moment,
        second_moment,
    )
    outer_grad = total.astype(f32)
    moment_new = beta_first * first_moment[0] + (1.0 - beta_first) * grad
    second_new = beta_second * second_moment[0] + (1.0 - beta_second) * grad * grad
    new_momentum = nesterov_factor * outer_momentum + outer_grad
    base_value = base_gate.astype(jnp.float32)
    new_base = base_value - outer_rate * (outer_grad + nesterov_factor * new_momentum)
    return (new_base, new_momentum, moment_new[None], second_new[None])


def solution(mesh):
    in_specs = (
        P("rep", "fsdp", None),
        P("rep", "fsdp", None),
        P("rep", "fsdp", None),
        P("rep", "fsdp", None),
        P("rep", "fsdp", None),
        P("fsdp", None),
        P("rep", "fsdp", None),
        P("rep", "fsdp", None),
        P("fsdp", None),
    )
    out_specs = (P("fsdp", None), P("fsdp", None), P("rep", "fsdp", None), P("rep", "fsdp", None))
    return jax.shard_map(
        on_device, mesh=mesh, in_specs=in_specs, out_specs=out_specs, check_vma=False
    )
```

time: 101 us -> 87.9 us (0.87)
  the two profiles are of different devices: /device:TPU:8 before, /device:TPU:2 now
where the time goes in v2:
time: 87.9 us; the launch traced here: 87.7 us
  Pallas kernels  83.6 us (95%)
  other arithmetic  3.36 us (4%)
    pallas_call x1, Pallas kernels, on_device(): pl.pallas_call(kernel, out_shape=[jax.ShapeDtypeStruct((UNITS, D), f32),...  83.6 us
    broadcast_in_dim x1, other arithmetic, on_device(): return (new_base, new_momentum, moment_new[None], second_new[None])  2.25 us

profile of v2, /device:TPU:2, one launch (start us, length us, event | category | flops | bytes accessed | tf_op | source)
XLA Modules:
  0.0 87.7 jit_solution(8174422530318389819)
XLA Ops:
  0.6 0.0 copy-start
  0.6 0.0 copy-start.1
  0.7 83.6 %window.1 = (f32[64,2048]{1,0:T(8,128)}, bf16[64,2048]{1,0:T(8,128)(2,1)}) custom-call(bf16[1,32,2048]{2,1,0:T(8,128)(2,1)} %tokens.1, bf16[1,32,2048]{2,1,0:T(8,128)(2,1)} %grads.1, bf16[1,64,2048]{2,1,0:T(8,128)(2,1)} %gate.1, bf16[1,64,2048]{2,1,0:T(8,128)(2,1)} %up.1, bf16[1,64,2048]{2,1,0:T(8,128)(2,1)} %down.1, bf16[64,2048]{1,0:T(8,128)(2,1)} %base.1, ...), custom_call_target="tpu_custom_call" | custom-call | tf_op jit(solution)/shard_map/window/pallas_call | solution.py:256
  84.3 0.0 copy-done
  84.3 0.0 copy-done.1
  84.3 0.0 copy-start.2
  84.3 0.0 copy-start.3
  84.3 0.0 copy-start.4
  84.3 2.3 %fusion.3 = (f32[1,64,2048]{2,1,0:T(8,128)}, f32[1,64,2048]{2,1,0:T(8,128)}) fusion(f32[64,2048]{1,0:T(8,128)} %get-tuple-element.7, f32[1,64,2048]{2,1,0:T(8,128)S(1)} %copy-done.1, f32[1,64,2048]{2,1,0:T(8,128)S(1)} %copy-done), kind=kLoop, calls=%fused_computation.6 | loop fusion | flops 917504 | bytes 2621440 | tf_op jit(solution)/shard_map/broadcast_in_dim | solution.py:313
  86.6 0.0 copy-done.2
  86.6 0.0 copy-done.3
  86.6 0.0 copy-done.4
  86.6 1.1 %fusion.1 = (f32[64,2048]{1,0:T(8,128)}, f32[64,2048]{1,0:T(8,128)}) fusion(bf16[64,2048]{1,0:T(8,128)(2,1)S(1)} %copy-done.4, bf16[64,2048]{1,0:T(8,128)(2,1)S(1)} %copy-done.2, f32[64,2048]{1,0:T(8,128)S(1)} %copy-done.3), kind=kLoop, calls=%fused_computation.4 | loop fusion | flops 1048576 | bytes 2097152 | tf_op jit(solution)/shard_map/sub | solution.py:312
Async XLA Ops:
  0.6 83.7 %copy-start = (f32[1,64,2048]{2,1,0:T(8,128)S(1)}, f32[1,64,2048]{2,1,0:T(8,128)}, u32[]{:S(2)}) copy-start(f32[1,64,2048]{2,1,0:T(8,128)} %first.1) | copy-start | bytes 1572868
  0.6 83.7 %copy-start.1 = (f32[1,64,2048]{2,1,0:T(8,128)S(1)}, f32[1,64,2048]{2,1,0:T(8,128)}, u32[]{:S(2)}) copy-start(f32[1,64,2048]{2,1,0:T(8,128)} %second.1) | copy-start | bytes 1572868
  84.3 2.3 %copy-start.2 = (bf16[64,2048]{1,0:T(8,128)(2,1)S(1)}, bf16[64,2048]{1,0:T(8,128)(2,1)}, u32[]{:S(2)}) copy-start(bf16[64,2048]{1,0:T(8,128)(2,1)} %base.1) | copy-start | bytes 786436
  84.3 2.3 %copy-start.3 = (f32[64,2048]{1,0:T(8,128)S(1)}, f32[64,2048]{1,0:T(8,128)}, u32[]{:S(2)}) copy-start(f32[64,2048]{1,0:T(8,128)} %param.17) | copy-start | bytes 1572868
  84.3 2.3 %copy-start.4 = (bf16[64,2048]{1,0:T(8,128)(2,1)S(1)}, bf16[64,2048]{1,0:T(8,128)(2,1)}, u32[]{:S(2)}) copy-start(bf16[64,2048]{1,0:T(8,128)(2,1)} %get-tuple-element.6) | copy-start | bytes 786436

commit v3 on v2

--- a/solution.py
+++ b/solution.py
@@ -21,7 +21,10 @@
 NZ, NY, REP = 8, 4, 8
 ROWS, UNITS, D = 32, 64, 2048
 SLOT = 4 * ROWS
-CHUNK = 16
+PIECE = 16
+PIECES = 4
+Y_FIRST = 3
+CHUNK = 32
 N_CHUNK = UNITS // CHUNK
 COLS = D // REP
 
@@ -40,8 +43,8 @@
 def kernel(
     tokens, grads, gate, up, down, base, first, second,
     grad_out, total_out,
-    xg, wp, wd, acc, base_v, first_v, second_v, gsend, grecv, grad_v, diff, diff_b, rs, ag,
-    load_sem, zs, zr, cs, cr, ys, yr, ws, wr, gs, gr, ss, sr, as_, ar, out_sem,
+    xg, wp, wd, held_v, acc, base_v, first_v, second_v, gsend, grecv, grad_v, diff, diff_b, rs, ag,
+    load_sem, zs, zr, cs, cr, ys, yr, ls, lr, ws, wr, gs, gr, ss, sr, as_, ar, out_sem,
 ):
     rep = lax.axis_index("rep")
     me = lax.axis_index("fsdp")
@@ -89,97 +92,161 @@
     def wait_bytes(ref, sem):
         pltpu.make_async_copy(ref, ref, sem).wait()
 
-    def shard(kind, slot, yy, cc):
-        return xg.at[kind, pl.ds(slot * SLOT + yy * 2 * ROWS + cc * ROWS, ROWS)]
-
-    def z_copy(way, yy, hops, kind):
+    def shard(slot, yy, cc, p):
+        row = slot * SLOT + yy * 2 * ROWS + cc * ROWS + p % 2 * PIECE
+        return xg.at[p // 2, pl.ds(row, PIECE)]
+
+    def goes(way, yy, hops, p):
+        if yy == 1 and p >= Y_FIRST:
+            return False
+        return hops < NZ // 2 or (hops == NZ // 2 and (p >= (PIECES - yy) // 2) == way)
+
+    def z_copy(way, yy, hops, p):
         return remote(
-            shard(kind, place(way, hops - 1), yy, 0),
-            shard(kind, place(way, hops), yy, 0),
+            shard(place(way, hops - 1), yy, 0, p),
+            shard(place(way, hops), yy, 0, p),
             zs,
-            zr.at[way, yy, hops - 1, kind],
+            zr.at[way, yy, hops - 1, p],
             z_next[way],
         )
 
-    def core_copy(slot, yy, kind):
-        return remote(shard(kind, slot, yy, 0), shard(kind, slot, yy, 1), cs, cr.at[slot], sibling)
-
-    def y_copy(kind):
-        return remote(shard(kind, 0, 0, 0), shard(kind, 0, 1, 0), ys, yr.at[kind], token_pair)
+    def core_copy(slot, yy, p):
+        return remote(shard(slot, yy, 0, p), shard(slot, yy, 1, p), cs, cr.at[slot], sibling)
+
+    def y_copy(p):
+        return remote(shard(0, 0, 0, p), shard(0, 1, 0, p), ys, yr.at[p], token_pair)
+
+    def late_copy(slot):
+        return remote(shard(slot, 0, 0, Y_FIRST), shard(slot, 1, 0, Y_FIRST), ls, lr.at[slot], token_pair)
 
     def w_copy(i):
         ref, row = ((wp, 0), (wp, 2 * UNITS), (wd, 0))[i]
-        return remote(ref.at[pl.ds(row, UNITS)], ref.at[pl.ds(row + UNITS, UNITS)], ws, wr, weight_pair)
-
-    for kind in range(2):
-        y_copy(kind).start()
+        return remote(ref.at[pl.ds(row, UNITS)], ref.at[pl.ds(row + UNITS, UNITS)], ws, wr.at[i // 2], weight_pair)
+
+    order = (*range(Y_FIRST, PIECES), *range(Y_FIRST))
+    for p in order:
+        if p < Y_FIRST:
+            y_copy(p).start()
         for way in range(2):
-            z_copy(way, 0, 1, kind).start()
+            z_copy(way, 0, 1, p).start()
+    late_copy(0).start()
     for i in range(3):
         w_copy(i).start()
-    for kind in range(2):
-        core_copy(0, 0, kind).start()
+    for p in range(PIECES):
+        core_copy(0, 0, p).start()
 
     def arrive(yy, hops):
-        for kind in range(2):
+        for p in order:
             for way in range(2):
-                if hops == NZ // 2 and kind != way:
+                if not goes(way, yy, hops, p):
                     continue
-                z_copy(way, yy, hops, kind).wait_recv()
-                if hops + 1 < NZ // 2 or (hops + 1 == NZ // 2 and kind == way):
-                    z_copy(way, yy, hops + 1, kind).start()
-                core_copy(place(way, hops), yy, kind).start()
+                slot = place(way, hops)
+                z_copy(way, yy, hops, p).wait_recv()
+                if goes(way, yy, hops + 1, p):
+                    z_copy(way, yy, hops + 1, p).start()
+                if p >= Y_FIRST:
+                    late_copy(slot).start()
+                core_copy(slot, yy, p).start()
+
+    def arrive_y():
+        for p in range(Y_FIRST):
+            y_copy(p).wait_recv()
+            for way in range(2):
+                z_copy(way, 1, 1, p).start()
+            core_copy(0, 1, p).start()
+
+    def arrive_late(hops):
+        for way in range(2):
+            if goes(way, 0, hops, Y_FIRST) and (hops > 0 or way == 0):
+                slot = place(way, hops)
+                late_copy(slot).wait_recv()
+                core_copy(slot, 1, Y_FIRST).start()
 
     nt = (((1,), (1,)), ((), ()))
 
-    def slopes(slot, slots):
+    def settle(slot, slots):
         for s in range(slot, slot + slots):
             wait_bytes(xg.at[0, pl.ds(0, SLOT)], cr.at[s])
+
+    def gain(slot, slots, unit, units):
+        x = xg[0, pl.ds(slot * SLOT, slots * SLOT)]
+        if units == 2 * UNITS:
+            both = lax.dot_general(wp[...], x, nt, preferred_element_type=jnp.float32) * in_scale
+            pre, lin = both[:units], both[units:]
+        else:
+            pre = lax.dot_general(wp[pl.ds(unit, units)], x, nt, preferred_element_type=jnp.float32) * in_scale
+            lin = lax.dot_general(wp[pl.ds(2 * UNITS + unit, units)], x, nt, preferred_element_type=jnp.float32) * in_scale
+        sig = jax.nn.sigmoid(pre)
+        return lin, sig, 1.0 + pre * (1.0 - sig)
+
+    def slope(slot, slots, unit, units, held):
         rows = pl.ds(slot * SLOT, slots * SLOT)
-        x = xg[0, rows]
-        both = lax.dot_general(wp[...], x, nt, preferred_element_type=jnp.float32) * in_scale
-        pre, lin = both[: 2 * UNITS], both[2 * UNITS :]
+        back = lax.dot_general(wd[pl.ds(unit, units)], xg[1, rows], nt, preferred_element_type=jnp.float32) * out_scale
+        lin, sig, rest = held
+        dpre = (back * lin * sig * rest).astype(jnp.bfloat16)
+        return jnp.dot(dpre, xg[0, rows], preferred_element_type=jnp.float32)
+
+    def partial(slot, slots, unit, units):
+        return slope(slot, slots, unit, units, gain(slot, slots, unit, units))
+
+    def early(slot, slots):
+        settle(slot, slots)
+        lin, sig, rest = gain(slot, slots, 0, 2 * UNITS)
+        cols = pl.ds(slot * SLOT, slots * SLOT)
+        held_v[:, cols] = lin * sig * rest
+
+    def late(slot, slots, begin=False):
+        rows = pl.ds(slot * SLOT, slots * SLOT)
         back = lax.dot_general(wd[...], xg[1, rows], nt, preferred_element_type=jnp.float32) * out_scale
-        sig = jax.nn.sigmoid(pre)
-        return (back * lin * sig * (1.0 + pre * (1.0 - sig))).astype(jnp.bfloat16), x
-
-    def block(slot, slots, begin=False):
-        dpre, x = slopes(slot, slots)
-        part = jnp.dot(dpre, x, preferred_element_type=jnp.float32)
+        dpre = (back * held_v[:, rows]).astype(jnp.bfloat16)
+        part = jnp.dot(dpre, xg[0, rows], preferred_element_type=jnp.float32)
         if begin:
             acc[...] = part
         else:
             acc[...] += part
 
+    def block(slot, slots, begin=False):
+        settle(slot, slots)
+        part = partial(slot, slots, 0, 2 * UNITS)
+        if begin:
+            acc[...] = part
+        else:
+            acc[...] += part
+
     arrive(0, 1)
     arrive(0, 2)
-    for kind in range(2):
-        y_copy(kind).wait_recv()
-        for way in range(2):
-            z_copy(way, 1, 1, kind).start()
-        core_copy(0, 1, kind).start()
+    arrive_y()
+    arrive_late(0)
+    arrive(0, 3)
+    arrive_late(1)
     arrive(1, 1)
-    arrive(0, 3)
+    arrive(0, 4)
+    arrive_late(2)
+    wait_bytes(wd, wr.at[0])
+    early(0, 1)
     arrive(1, 2)
-    arrive(0, 4)
-    wait_bytes(wp.at[pl.ds(0, 3 * UNITS)], wr)
-    block(0, 1, True)
-    block(2, 2)
-    block(4, 2)
+    early(2, 2)
+    early(4, 2)
+    w_copy(2).wait_recv()
+    late(0, 1, True)
+    arrive_late(3)
     arrive(1, 3)
+    late(2, 2)
+    late(4, 2)
     block(6, 2)
+    arrive_late(4)
     arrive(1, 4)
 
     def g_copy(c):
         rows = pl.ds(c * CHUNK, CHUNK)
         return remote(gsend.at[rows], grecv.at[rows], gs, gr.at[c], weight_pair)
 
-    dpre, x = slopes(1, 1)
-    part = jnp.dot(dpre[UNITS:], x, preferred_element_type=jnp.float32)
+    settle(1, 1)
+    part = partial(1, 1, UNITS, UNITS)
     gsend[...] = (acc[pl.ds(UNITS, UNITS)] + part).astype(jnp.bfloat16)
     for c in range(N_CHUNK):
         g_copy(c).start()
-    acc[pl.ds(0, UNITS)] += jnp.dot(dpre[:UNITS], x, preferred_element_type=jnp.float32)
+    acc[pl.ds(0, UNITS)] += partial(1, 1, 0, UNITS)
     for load in loads[5:]:
         load.wait()
 
@@ -229,9 +296,11 @@
         wait_bytes(ag.at[rows, pl.ds(0, D - COLS)], ar.at[c])
         pltpu.make_async_copy(ag.at[rows], total_out.at[rows], out_sem.at[1]).start()
 
-    wait_bytes(xg.at[0, pl.ds(0, 28 * ROWS)], zs)
+    z_sends = sum(goes(w, yy, h, p) for w in range(2) for yy in range(2) for h in range(1, 5) for p in range(PIECES))
+    wait_bytes(xg.at[0, pl.ds(0, z_sends * PIECE)], zs)
     wait_bytes(xg.at[0], cs)
-    wait_bytes(xg.at[0, pl.ds(0, 2 * ROWS)], ys)
+    wait_bytes(xg.at[0, pl.ds(0, Y_FIRST * PIECE)], ys)
+    wait_bytes(xg.at[0, pl.ds(0, NZ * PIECE)], ls)
     wait_bytes(wp.at[pl.ds(0, 3 * UNITS)], ws)
     wait_bytes(gsend, gs)
     wait_bytes(diff_b.at[:, pl.ds(0, D - COLS)], ss)
@@ -262,6 +331,7 @@
             pltpu.VMEM((2, NZ * SLOT, D), bf16),
             pltpu.VMEM((4 * UNITS, D), bf16),
             pltpu.VMEM((2 * UNITS, D), bf16),
+            pltpu.VMEM((2 * UNITS, NZ * SLOT), f32),
             pltpu.VMEM((2 * UNITS, D), f32),
             pltpu.VMEM((UNITS, D), bf16),
             pltpu.VMEM((UNITS, D), f32),
@@ -275,13 +345,15 @@
             pltpu.VMEM((UNITS, D), bf16),
             dma((4,)),
             dma,
-            dma((2, 2, NZ // 2, 2)),
+            dma((2, 2, NZ // 2, PIECES)),
             dma,
             dma((NZ,)),
             dma,
+            dma((Y_FIRST,)),
+            dma,
+            dma((NZ,)),
+            dma,
             dma((2,)),
-            dma,
-            dma,
             dma,
             dma((N_CHUNK,)),
             dma,

time: 87.9 us -> 82.7 us (0.941)
  the two profiles are of different devices: /device:TPU:2 before, /device:TPU:16 now
where the time goes in v3:
time: 82.7 us; the launch traced here: 82.5 us
  Pallas kernels  78.4 us (95%)
  other arithmetic  3.36 us (4%)
    pallas_call x1, Pallas kernels, on_device(): pl.pallas_call(kernel, out_shape=[jax.ShapeDtypeStruct((UNITS, D), f32),...  78.4 us
    broadcast_in_dim x1, other arithmetic, on_device(): return (new_base, new_momentum, moment_new[None], second_new[None])  2.25 us

profile of v3, /device:TPU:16, one launch (start us, length us, event | category | flops | bytes accessed | tf_op | source)
XLA Modules:
  0.0 82.5 jit_solution(1365907710497424836)
XLA Ops:
  0.6 0.0 copy-start
  0.6 0.0 copy-start.1
  0.7 78.4 %window.1 = (f32[64,2048]{1,0:T(8,128)}, bf16[64,2048]{1,0:T(8,128)(2,1)}) custom-call(bf16[1,32,2048]{2,1,0:T(8,128)(2,1)} %tokens.1, bf16[1,32,2048]{2,1,0:T(8,128)(2,1)} %grads.1, bf16[1,64,2048]{2,1,0:T(8,128)(2,1)} %gate.1, bf16[1,64,2048]{2,1,0:T(8,128)(2,1)} %up.1, bf16[1,64,2048]{2,1,0:T(8,128)(2,1)} %down.1, bf16[64,2048]{1,0:T(8,128)(2,1)} %base.1, ...), custom_call_target="tpu_custom_call" | custom-call | tf_op jit(solution)/shard_map/window/pallas_call | solution.py:325
  79.1 0.0 copy-done
  79.1 0.0 copy-done.1
  79.1 0.0 copy-start.2
  79.1 0.0 copy-start.3
  79.1 0.0 copy-start.4
  79.2 2.3 %fusion.3 = (f32[1,64,2048]{2,1,0:T(8,128)}, f32[1,64,2048]{2,1,0:T(8,128)}) fusion(f32[64,2048]{1,0:T(8,128)} %get-tuple-element.7, f32[1,64,2048]{2,1,0:T(8,128)S(1)} %copy-done.1, f32[1,64,2048]{2,1,0:T(8,128)S(1)} %copy-done), kind=kLoop, calls=%fused_computation.6 | loop fusion | flops 917504 | bytes 2621440 | tf_op jit(solution)/shard_map/broadcast_in_dim | solution.py:385
  81.4 0.0 copy-done.2
  81.4 0.0 copy-done.3
  81.4 0.0 copy-done.4
  81.4 1.1 %fusion.1 = (f32[64,2048]{1,0:T(8,128)}, f32[64,2048]{1,0:T(8,128)}) fusion(bf16[64,2048]{1,0:T(8,128)(2,1)S(1)} %copy-done.4, bf16[64,2048]{1,0:T(8,128)(2,1)S(1)} %copy-done.2, f32[64,2048]{1,0:T(8,128)S(1)} %copy-done.3), kind=kLoop, calls=%fused_computation.4 | loop fusion | flops 1048576 | bytes 2097152 | tf_op jit(solution)/shard_map/sub | solution.py:384
Async XLA Ops:
  0.6 78.5 %copy-start = (f32[1,64,2048]{2,1,0:T(8,128)S(1)}, f32[1,64,2048]{2,1,0:T(8,128)}, u32[]{:S(2)}) copy-start(f32[1,64,2048]{2,1,0:T(8,128)} %first.1) | copy-start | bytes 1572868
  0.6 78.5 %copy-start.1 = (f32[1,64,2048]{2,1,0:T(8,128)S(1)}, f32[1,64,2048]{2,1,0:T(8,128)}, u32[]{:S(2)}) copy-start(f32[1,64,2048]{2,1,0:T(8,128)} %second.1) | copy-start | bytes 1572868
  79.1 2.3 %copy-start.2 = (bf16[64,2048]{1,0:T(8,128)(2,1)S(1)}, bf16[64,2048]{1,0:T(8,128)(2,1)}, u32[]{:S(2)}) copy-start(bf16[64,2048]{1,0:T(8,128)(2,1)} %base.1) | copy-start | bytes 786436
  79.1 2.3 %copy-start.3 = (f32[64,2048]{1,0:T(8,128)S(1)}, f32[64,2048]{1,0:T(8,128)}, u32[]{:S(2)}) copy-start(f32[64,2048]{1,0:T(8,128)} %param.17) | copy-start | bytes 1572868
  79.1 2.3 %copy-start.4 = (bf16[64,2048]{1,0:T(8,128)(2,1)S(1)}, bf16[64,2048]{1,0:T(8,128)(2,1)}, u32[]{:S(2)}) copy-start(bf16[64,2048]{1,0:T(8,128)(2,1)} %get-tuple-element.6) | copy-start | bytes 786436

commit v4 on v3

--- a/solution.py
+++ b/solution.py
@@ -43,8 +43,8 @@
 def kernel(
     tokens, grads, gate, up, down, base, first, second,
     grad_out, total_out,
-    xg, wp, wd, held_v, acc, base_v, first_v, second_v, gsend, grecv, grad_v, diff, diff_b, rs, ag,
-    load_sem, zs, zr, cs, cr, ys, yr, ls, lr, ws, wr, gs, gr, ss, sr, as_, ar, out_sem,
+    xg, wp, wd, held_v, acc, base_v, first_v, second_v, gsend, grecv, diff, diff_b, rs, ag,
+    load_sem, zs, zr, cs, cr, ys, yr, ls, lr, ws, wr, gs, gr, ss, sr, as_, ar,
 ):
     rep = lax.axis_index("rep")
     me = lax.axis_index("fsdp")
@@ -275,7 +275,7 @@
         rows = pl.ds(c * CHUNK, CHUNK)
         g_copy(c).wait_recv()
         grad = (acc[rows] + grecv[rows].astype(jnp.float32)) * in_scale
-        grad_v[rows] = grad
+        grad_out[rows] = grad
         moment_new = beta_first * first_v[rows] + (1.0 - beta_first) * grad
         second_new = beta_second * second_v[rows] + (1.0 - beta_second) * grad * grad
         direction = moment_new / bias_first / (jnp.sqrt(second_new / bias_second) + adam_floor)
@@ -286,7 +286,6 @@
         diff_b[rows] = difference.astype(jnp.bfloat16)
         for k in range(1, REP):
             rs_copy(c, k).start()
-        pltpu.make_async_copy(grad_v.at[rows], grad_out.at[rows], out_sem.at[0]).start()
         if c > 0:
             sum_chunk(c - 1)
     sum_chunk(N_CHUNK - 1)
@@ -294,7 +293,7 @@
     for c in range(N_CHUNK):
         rows = pl.ds(c * CHUNK, CHUNK)
         wait_bytes(ag.at[rows, pl.ds(0, D - COLS)], ar.at[c])
-        pltpu.make_async_copy(ag.at[rows], total_out.at[rows], out_sem.at[1]).start()
+        total_out[rows] = ag[rows]
 
     z_sends = sum(goes(w, yy, h, p) for w in range(2) for yy in range(2) for h in range(1, 5) for p in range(PIECES))
     wait_bytes(xg.at[0, pl.ds(0, z_sends * PIECE)], zs)
@@ -305,8 +304,6 @@
     wait_bytes(gsend, gs)
     wait_bytes(diff_b.at[:, pl.ds(0, D - COLS)], ss)
     wait_bytes(diff_b.at[:, pl.ds(0, D - COLS)], as_)
-    wait_bytes(grad_v, out_sem.at[0])
-    wait_bytes(ag, out_sem.at[1])
 
 
 def on_device(
@@ -324,9 +321,9 @@
     f32, bf16 = jnp.float32, jnp.bfloat16
     grad, total = pl.pallas_call(
         kernel,
-        out_shape=[jax.ShapeDtypeStruct((UNITS, D), f32), jax.ShapeDtypeStruct((UNITS, D), bf16)],
+        out_shape=[pltpu.VMEM((UNITS, D), f32), pltpu.VMEM((UNITS, D), bf16)],
         in_specs=[pl.BlockSpec(memory_space=pl.ANY)] * 8,
-        out_specs=[pl.BlockSpec(memory_space=pl.ANY)] * 2,
+        out_specs=[pl.BlockSpec(memory_space=pltpu.VMEM)] * 2,
         scratch_shapes=[
             pltpu.VMEM((2, NZ * SLOT, D), bf16),
             pltpu.VMEM((4 * UNITS, D), bf16),
@@ -339,7 +336,6 @@
             pltpu.VMEM((UNITS, D), bf16),
             pltpu.VMEM((UNITS, D), bf16),
             pltpu.VMEM((UNITS, D), f32),
-            pltpu.VMEM((UNITS, D), f32),
             pltpu.VMEM((UNITS, D), bf16),
             pltpu.VMEM((REP - 1, UNITS, COLS), bf16),
             pltpu.VMEM((UNITS, D), bf16),
@@ -360,10 +356,9 @@
             dma((N_CHUNK,)),
             dma,
             dma((N_CHUNK,)),
-            dma((2,)),
         ],
         compiler_params=pltpu.CompilerParams(
-            collective_id=0, has_side_effects=True, vmem_limit_bytes=60 * 2**20
+            collective_id=0, has_side_effects=True, vmem_limit_bytes=54 * 2**20
         ),
         name="window",
     )(

time: 82.7 us -> 81 us (0.979)
  other arithmetic: 3.36 us -> 2.24 us
    broadcast_in_dim x1, other arithmetic: 2.25 us -> 1.13 us  [on_device(): return (new_base, new_momentum, moment_new[None], second_new[None])]
where the time goes in v4:
time: 81 us; the launch traced here: 80.8 us
  Pallas kernels  77.8 us (96%)
  other arithmetic  2.24 us (3%)
    pallas_call x1, Pallas kernels, on_device(): pl.pallas_call(kernel, out_shape=[pltpu.VMEM((UNITS, D), f32), pltpu.VMEM...  77.8 us

profile of v4, /device:TPU:16, one launch (start us, length us, event | category | flops | bytes accessed | tf_op | source)
XLA Modules:
  0.0 80.8 jit_solution(13722536381239771618)
XLA Ops:
  0.6 0.0 copy-start
  0.6 0.0 copy-start.1
  0.7 77.8 %window.1 = (f32[64,2048]{1,0:T(8,128)S(1)}, bf16[64,2048]{1,0:T(8,128)(2,1)S(1)}) custom-call(bf16[1,32,2048]{2,1,0:T(8,128)(2,1)} %tokens.1, bf16[1,32,2048]{2,1,0:T(8,128)(2,1)} %grads.1, bf16[1,64,2048]{2,1,0:T(8,128)(2,1)} %gate.1, bf16[1,64,2048]{2,1,0:T(8,128)(2,1)} %up.1, bf16[1,64,2048]{2,1,0:T(8,128)(2,1)} %down.1, bf16[64,2048]{1,0:T(8,128)(2,1)} %base.1, ...), custom_call_target="tpu_custom_call" | custom-call | tf_op jit(solution)/shard_map/window/pallas_call | solution.py:322
  78.5 0.0 copy-done
  78.5 0.0 copy-done.1
  78.5 0.0 copy-start.2
  78.5 0.0 copy-start.3
  78.5 1.1 %fusion.3 = (f32[1,64,2048]{2,1,0:T(8,128)}, f32[1,64,2048]{2,1,0:T(8,128)}) fusion(f32[64,2048]{1,0:T(8,128)S(1)} %get-tuple-element.7, f32[1,64,2048]{2,1,0:T(8,128)S(1)} %copy-done.1, f32[1,64,2048]{2,1,0:T(8,128)S(1)} %copy-done), kind=kLoop, calls=%fused_computation.6 | loop fusion | flops 917504 | bytes 2621440 | tf_op jit(solution)/shard_map/broadcast_in_dim | solution.py:380
  79.6 0.0 copy-done.2
  79.6 0.1 copy-done.3
  79.7 1.1 %fusion.1 = (f32[64,2048]{1,0:T(8,128)}, f32[64,2048]{1,0:T(8,128)}) fusion(bf16[64,2048]{1,0:T(8,128)(2,1)S(1)} %get-tuple-element.6, bf16[64,2048]{1,0:T(8,128)(2,1)S(1)} %copy-done.2, f32[64,2048]{1,0:T(8,128)S(1)} %copy-done.3), kind=kLoop, calls=%fused_computation.4 | loop fusion | flops 1048576 | bytes 2097152 | tf_op jit(solution)/shard_map/sub | solution.py:379
Async XLA Ops:
  0.6 77.8 %copy-start = (f32[1,64,2048]{2,1,0:T(8,128)S(1)}, f32[1,64,2048]{2,1,0:T(8,128)}, u32[]{:S(2)}) copy-start(f32[1,64,2048]{2,1,0:T(8,128)} %first.1) | copy-start | bytes 1572868
  0.6 77.8 %copy-start.1 = (f32[1,64,2048]{2,1,0:T(8,128)S(1)}, f32[1,64,2048]{2,1,0:T(8,128)}, u32[]{:S(2)}) copy-start(f32[1,64,2048]{2,1,0:T(8,128)} %second.1) | copy-start | bytes 1572868
  78.5 1.2 %copy-start.2 = (bf16[64,2048]{1,0:T(8,128)(2,1)S(1)}, bf16[64,2048]{1,0:T(8,128)(2,1)}, u32[]{:S(2)}) copy-start(bf16[64,2048]{1,0:T(8,128)(2,1)} %base.1) | copy-start | bytes 786436
  78.5 1.2 %copy-start.3 = (f32[64,2048]{1,0:T(8,128)S(1)}, f32[64,2048]{1,0:T(8,128)}, u32[]{:S(2)}) copy-start(f32[64,2048]{1,0:T(8,128)} %param.17) | copy-start | bytes 1572868

commit v5 on v4

--- a/solution.py
+++ b/solution.py
@@ -60,6 +60,7 @@
     token_pair = at(z, y + 1 - 2 * (y % 2), core)
     weight_pair = at(z, (y + 3 + 2 * (y % 2)) % NY, core)
     peers = [((rep + k) % REP, me) for k in range(1, REP)]
+    far_first = (4, 3, 5, 2, 6, 1, 7)
 
     loads = [
         pltpu.make_async_copy(src, dst, load_sem.at[i])
@@ -111,7 +112,7 @@
         )
 
     def core_copy(slot, yy, p):
-        return remote(shard(slot, yy, 0, p), shard(slot, yy, 1, p), cs, cr.at[slot], sibling)
+        return remote(shard(slot, yy, 0, p), shard(slot, yy, 1, p), cs, cr.at[slot, p // 2], sibling)
 
     def y_copy(p):
         return remote(shard(0, 0, 0, p), shard(0, 1, 0, p), ys, yr.at[p], token_pair)
@@ -166,7 +167,8 @@
 
     def settle(slot, slots):
         for s in range(slot, slot + slots):
-            wait_bytes(xg.at[0, pl.ds(0, SLOT)], cr.at[s])
+            for kind in range(2):
+                wait_bytes(xg.at[0, pl.ds(0, SLOT // 2)], cr.at[s, kind])
 
     def gain(slot, slots, unit, units):
         x = xg[0, pl.ds(slot * SLOT, slots * SLOT)]
@@ -216,21 +218,21 @@
     arrive(0, 1)
     arrive(0, 2)
     arrive_y()
+    arrive(0, 3)
+    arrive(1, 1)
     arrive_late(0)
-    arrive(0, 3)
     arrive_late(1)
-    arrive(1, 1)
     arrive(0, 4)
-    arrive_late(2)
     wait_bytes(wd, wr.at[0])
     early(0, 1)
     arrive(1, 2)
+    arrive_late(2)
     early(2, 2)
     early(4, 2)
     w_copy(2).wait_recv()
     late(0, 1, True)
+    arrive(1, 3)
     arrive_late(3)
-    arrive(1, 3)
     late(2, 2)
     late(4, 2)
     block(6, 2)
@@ -241,14 +243,19 @@
         rows = pl.ds(c * CHUNK, CHUNK)
         return remote(gsend.at[rows], grecv.at[rows], gs, gr.at[c], weight_pair)
 
-    settle(1, 1)
-    part = partial(1, 1, UNITS, UNITS)
+    wait_bytes(xg.at[0, pl.ds(0, SLOT // 2)], cr.at[1, 0])
+    held = gain(1, 1, UNITS, UNITS)
+    wait_bytes(xg.at[0, pl.ds(0, SLOT // 2)], cr.at[1, 1])
+    part = slope(1, 1, UNITS, UNITS, held)
     gsend[...] = (acc[pl.ds(UNITS, UNITS)] + part).astype(jnp.bfloat16)
     for c in range(N_CHUNK):
         g_copy(c).start()
     acc[pl.ds(0, UNITS)] += partial(1, 1, 0, UNITS)
     for load in loads[5:]:
         load.wait()
+    own = pl.ds(0, UNITS)
+    acc[own] = acc[own] * in_scale
+    diff[...] = base_v[...].astype(jnp.float32) - wp[own].astype(jnp.float32) * (1.0 - inner_rate * decay_rate)
 
     mine = pl.ds(pl.multiple_of(rep * COLS, COLS), COLS)
 
@@ -268,23 +275,21 @@
         for k in range(1, REP):
             total += rs[k - 1, rows].astype(jnp.float32)
         ag[rows, mine] = (total / REP).astype(jnp.bfloat16)
-        for k in range(1, REP):
+        for k in far_first:
             ag_copy(c, k).start()
 
     for c in range(N_CHUNK):
         rows = pl.ds(c * CHUNK, CHUNK)
         g_copy(c).wait_recv()
-        grad = (acc[rows] + grecv[rows].astype(jnp.float32)) * in_scale
+        grad = acc[rows] + grecv[rows].astype(jnp.float32) * in_scale
         grad_out[rows] = grad
         moment_new = beta_first * first_v[rows] + (1.0 - beta_first) * grad
         second_new = beta_second * second_v[rows] + (1.0 - beta_second) * grad * grad
-        direction = moment_new / bias_first / (jnp.sqrt(second_new / bias_second) + adam_floor)
-        gate_value = wp[rows].astype(jnp.float32)
-        inner = gate_value * (1.0 - inner_rate * decay_rate) - inner_rate * direction
-        difference = base_v[rows].astype(jnp.float32) - inner
+        direction = moment_new * (1.0 / bias_first) / (jnp.sqrt(second_new * (1.0 / bias_second)) + adam_floor)
+        difference = diff[rows] + inner_rate * direction
         diff[rows] = difference
         diff_b[rows] = difference.astype(jnp.bfloat16)
-        for k in range(1, REP):
+        for k in far_first:
             rs_copy(c, k).start()
         if c > 0:
             sum_chunk(c - 1)
@@ -343,7 +348,7 @@
             dma,
             dma((2, 2, NZ // 2, PIECES)),
             dma,
-            dma((NZ,)),
+            dma((NZ, 2)),
             dma,
             dma((Y_FIRST,)),
             dma,

time: 81 us -> 81 us (level)
  no operation moved by 1% of the time
where the time goes in v5:
time: 81 us; the launch traced here: 80.9 us
  Pallas kernels  77.9 us (96%)
  other arithmetic  2.24 us (3%)
    pallas_call x1, Pallas kernels, on_device(): pl.pallas_call(kernel, out_shape=[pltpu.VMEM((UNITS, D), f32), pltpu.VMEM...  77.9 us

profile of v5, /device:TPU:16, one launch (start us, length us, event | category | flops | bytes accessed | tf_op | source)
XLA Modules:
  0.0 80.9 jit_solution(13796669563552978616)
XLA Ops:
  0.6 0.0 copy-start
  0.6 0.0 copy-start.1
  0.7 77.9 %window.1 = (f32[64,2048]{1,0:T(8,128)S(1)}, bf16[64,2048]{1,0:T(8,128)(2,1)S(1)}) custom-call(bf16[1,32,2048]{2,1,0:T(8,128)(2,1)} %tokens.1, bf16[1,32,2048]{2,1,0:T(8,128)(2,1)} %grads.1, bf16[1,64,2048]{2,1,0:T(8,128)(2,1)} %gate.1, bf16[1,64,2048]{2,1,0:T(8,128)(2,1)} %up.1, bf16[1,64,2048]{2,1,0:T(8,128)(2,1)} %down.1, bf16[64,2048]{1,0:T(8,128)(2,1)} %base.1, ...), custom_call_target="tpu_custom_call" | custom-call | tf_op jit(solution)/shard_map/window/pallas_call | solution.py:327
  78.5 0.0 copy-done
  78.5 0.0 copy-done.1
  78.5 0.0 copy-start.2
  78.5 0.0 copy-start.3
  78.6 1.1 %fusion.3 = (f32[1,64,2048]{2,1,0:T(8,128)}, f32[1,64,2048]{2,1,0:T(8,128)}) fusion(f32[64,2048]{1,0:T(8,128)S(1)} %get-tuple-element.7, f32[1,64,2048]{2,1,0:T(8,128)S(1)} %copy-done.1, f32[1,64,2048]{2,1,0:T(8,128)S(1)} %copy-done), kind=kLoop, calls=%fused_computation.6 | loop fusion | flops 917504 | bytes 2621440 | tf_op jit(solution)/shard_map/broadcast_in_dim | solution.py:385
  79.7 0.0 copy-done.2
  79.7 0.1 copy-done.3
  79.8 1.1 %fusion.1 = (f32[64,2048]{1,0:T(8,128)}, f32[64,2048]{1,0:T(8,128)}) fusion(bf16[64,2048]{1,0:T(8,128)(2,1)S(1)} %get-tuple-element.6, bf16[64,2048]{1,0:T(8,128)(2,1)S(1)} %copy-done.2, f32[64,2048]{1,0:T(8,128)S(1)} %copy-done.3), kind=kLoop, calls=%fused_computation.4 | loop fusion | flops 1048576 | bytes 2097152 | tf_op jit(solution)/shard_map/sub | solution.py:384
Async XLA Ops:
  0.6 77.9 %copy-start = (f32[1,64,2048]{2,1,0:T(8,128)S(1)}, f32[1,64,2048]{2,1,0:T(8,128)}, u32[]{:S(2)}) copy-start(f32[1,64,2048]{2,1,0:T(8,128)} %first.1) | copy-start | bytes 1572868
  0.6 77.9 %copy-start.1 = (f32[1,64,2048]{2,1,0:T(8,128)S(1)}, f32[1,64,2048]{2,1,0:T(8,128)}, u32[]{:S(2)}) copy-start(f32[1,64,2048]{2,1,0:T(8,128)} %second.1) | copy-start | bytes 1572868
  78.5 1.2 %copy-start.2 = (bf16[64,2048]{1,0:T(8,128)(2,1)S(1)}, bf16[64,2048]{1,0:T(8,128)(2,1)}, u32[]{:S(2)}) copy-start(bf16[64,2048]{1,0:T(8,128)(2,1)} %base.1) | copy-start | bytes 786436
  78.5 1.2 %copy-start.3 = (f32[64,2048]{1,0:T(8,128)S(1)}, f32[64,2048]{1,0:T(8,128)}, u32[]{:S(2)}) copy-start(f32[64,2048]{1,0:T(8,128)} %param.17) | copy-start | bytes 1572868
